TPU v7x, 512 devices: a whole 4x4x16 slice. The times are simulated.
512 devices in a mesh: fiber: 32 (over z, core), row: 16 (over x, y).
Axes of the slice: x: 4, y: 4, z: 16, core: 2. Of those that a mesh axis runs over, the one named last changes fastest.
Arguments:
- deltas: float32 [32, 2048, 2048], P('fiber', 'row'), may hold values from -6 to 6
- row_sketch: float32 [2048, 320], P('row'), may hold values from -0.125 to 0.125
- slab_sketch: float32 [32, 320], P('fiber'), may hold values from -6 to 6
- core_sketch: float32 [320, 320], replicated, may hold values from -0.3125 to 0.3125
- slab_sketch_two: float32 [32, 320], P('fiber'), may hold values from -6 to 6
- ranks: int32 [2], replicated, may hold values from 160 to 320
Outputs:
- core: float32 [32, 320, 320], P('fiber', None, 'row')
All inputs are finite; a program needn't handle non-finite values.
Results may differ from a plain program's by a relative error of at most 0.00028.
Values sent between devices are 32-bit elements; how exact they have to be, the bound alone decides.
A program may use at most 64 MiB of HBM per device.

v0:
```python
import jax
import jax.numpy as jnp
from jax import lax
from jax.sharding import PartitionSpec as P

HIGH = lax.Precision.HIGHEST


def gram_of(block):
    return jnp.dot(block.T, block, precision=HIGH, preferred_element_type=jnp.float32)


def cholesky_pass(block, gram):
    lower = jnp.linalg.cholesky(gram)
    return lax.linalg.triangular_solve(lower, block, left_side=False, lower=True, transpose_a=True)


def orthonormal(block):
    return cholesky_pass(block, lax.psum(gram_of(block), "row"))


def local(deltas, row_sketch, slab_sketch, core_sketch, slab_sketch_two, ranks):
    sketch = core_sketch.shape[0]
    columns = jnp.arange(sketch, dtype=jnp.int32)
    regrouped = lax.all_to_all(deltas, "row", split_axis=2, concat_axis=1, tiled=True)
    folded = jnp.einsum(
        "mpq,qs->mps",
        deltas,
        lax.all_gather(row_sketch, "row", axis=0, tiled=True),
        precision=HIGH,
        preferred_element_type=jnp.float32,
    )
    local_one = jnp.einsum(
        "mps,ms->ps", folded, slab_sketch, precision=HIGH, preferred_element_type=jnp.float32
    )
    sketch_one = lax.psum(local_one, "fiber")
    kept_one = jnp.where(columns[None, :] < ranks[0], orthonormal(sketch_one), jnp.float32(0.0))
    full_basis = lax.all_gather(kept_one, "row", axis=0, tiled=True)
    partial_value = jnp.einsum(
        "mpq,ps->qms", regrouped, full_basis, precision=HIGH, preferred_element_type=jnp.float32
    )
    mixed = jnp.einsum(
        "qms,st->qmt",
        partial_value,
        core_sketch,
        precision=HIGH,
        preferred_element_type=jnp.float32,
    )
    local_two = jnp.einsum(
        "qmt,mt->qt", mixed, slab_sketch_two, precision=HIGH, preferred_element_type=jnp.float32
    )
    sketch_two = lax.psum(local_two, "fiber")
    kept_two = jnp.where(columns[None, :] < ranks[1], orthonormal(sketch_two), jnp.float32(0.0))
    core_part = jnp.einsum(
        "qms,qt->mst", partial_value, kept_two, precision=HIGH, preferred_element_type=jnp.float32
    )
    return lax.psum_scatter(core_part, "row", scatter_dimension=2, tiled=True)


def solution(mesh):
    in_specs = (
        P("fiber", "row", None),
        P("row", None),
        P("fiber", None),
        P(),
        P("fiber", None),
        P(),
    )
    out_specs = P("fiber", None, "row")
    return jax.shard_map(local, mesh=mesh, in_specs=in_specs, out_specs=out_specs, check_vma=False)
```

profile of v0, /device:TPU:1, one launch (start us, length us, event | category | flops | bytes accessed | tf_op | source)
XLA Modules:
  0.0 1091.3 jit_solution(1602106488356091791)
XLA Ops:
  8.0 72.2 %all-gather.3.cloned.1.call-done = f32[2048,320]{0,1:T(8,128)} async-done(((f32[128,320]{0,1:T(8,128)}), f32[2048,320]{0,1:T(8,128)}) %all-gather.3.cloned.1.call-update) | async-done | bytes 2621456 | tf_op jit(solution)/shard_map/all_gather | solution.py:29
  80.2 4.9 fusion
  85.7 196.8 %all-reduce.10.cloned.1.call-done = f32[128,320]{0,1:T(8,128)} async-done(((f32[128,320]{0,1:T(8,128)}), f32[128,320]{0,1:T(8,128)}) %all-reduce.10.cloned.1.call-update) | async-done | bytes 163856 | tf_op jit(solution)/shard_map/psum | solution.py:36
  282.5 2.3 fusion.51
  285.8 113.0 %all-reduce.12.cloned.1.call-done = f32[320,320]{0,1:T(8,128)} async-done(((f32[320,320]{0,1:T(8,128)}), f32[320,320]{0,1:T(8,128)}) %all-reduce.12.cloned.1.call-update) | async-done | bytes 409616 | tf_op jit(solution)/shard_map/psum | solution.py:19
  401.1 11.7 %cholesky.214 = f32[128,128]{1,0:T(8,128)S(1)} custom-call(f32[128,128]{1,0:T(8,128)S(1)} %cholesky.324), custom_call_target="Cholesky" | custom-call | tf_op jit(solution)/shard_map/jit(cholesky)/cholesky | solution.py:14
  412.9 9.8 custom-call.20
  423.3 11.7 %cholesky.233 = f32[128,128]{1,0:T(8,128)S(1)} custom-call(f32[128,128]{1,0:T(8,128)S(1)} %cholesky.328), custom_call_target="Cholesky" | custom-call | tf_op jit(solution)/shard_map/jit(cholesky)/cholesky | solution.py:14
  435.0 10.0 custom-call.21
  445.4 5.8 cholesky.255
  454.7 4.1 while.4
  455.3 1.4 bitcast_dynamic-update-slice_fusion.4
  457.4 1.4 bitcast_dynamic-update-slice_fusion.4
  458.9 29.5 %custom-call.22 = f32[3,128,128]{1,2,0:T(8,128)S(1)} custom-call(f32[3,128,128]{2,1,0:T(8,128)S(1)} %pad_maximum_fusion), custom_call_target="InvertDiagBlocksLowerTriangular" | custom-call | tf_op jit(solution)/shard_map/triangular_solve/custom-call.2 | solution.py:15
  490.5 1.9 copy.29
  492.4 3.8 all-to-all-start
  496.3 14.6 %all-to-all-done = f32[1,128,2048]{1,0,2:T(1,128)S(1)} async-done(((f32[1,128,2048]{1,0,2:T(1,128)}), f32[1,128,2048]{1,0,2:T(1,128)S(1)}, u32[]{:S(2)}, u32[]{:S(2)}) %all-to-all-start) | async-done | bytes 1048608 | tf_op jit(solution)/shard_map/all_to_all | solution.py:25
  511.2 44.2 %all-gather.5.cloned.1.call-done = f32[2048,320]{0,1:T(8,128)} async-done(((f32[128,320]{0,1:T(8,128)}), f32[2048,320]{0,1:T(8,128)}) %all-gather.5.cloned.1.call-update) | async-done | bytes 2621456 | tf_op jit(solution)/shard_map/all_gather | solution.py:38
  555.4 3.9 convolution_bitcast_fusion.1
  559.3 1.7 convolution_multiply_fusion
  561.1 197.4 %all-reduce.14.cloned.1.call-done = f32[128,320]{0,1:T(8,128)} async-done(((f32[128,320]{0,1:T(8,128)}), f32[128,320]{0,1:T(8,128)}) %all-reduce.14.cloned.1.call-update) | async-done | bytes 163856 | tf_op jit(solution)/shard_map/psum | solution.py:52
  758.5 2.3 fusion.52
  761.9 112.7 %all-reduce.16.cloned.1.call-done = f32[320,320]{0,1:T(8,128)} async-done(((f32[320,320]{0,1:T(8,128)}), f32[320,320]{0,1:T(8,128)}) %all-reduce.16.cloned.1.call-update) | async-done | bytes 409616 | tf_op jit(solution)/shard_map/psum | solution.py:19
  877.0 11.7 %cholesky.271 = f32[128,128]{1,0:T(8,128)S(1)} custom-call(f32[128,128]{1,0:T(8,128)S(1)} %cholesky.332), custom_call_target="Cholesky" | custom-call | tf_op jit(solution)/shard_map/jit(cholesky)/cholesky | solution.py:14
  888.8 9.8 custom-call.23
  899.1 11.7 %cholesky.290 = f32[128,128]{1,0:T(8,128)S(1)} custom-call(f32[128,128]{1,0:T(8,128)S(1)} %cholesky.336), custom_call_target="Cholesky" | custom-call | tf_op jit(solution)/shard_map/jit(cholesky)/cholesky | solution.py:14
  912.2 10.0 custom-call.24
  922.6 5.8 cholesky.312
  931.1 4.1 while.5
  931.7 1.4 bitcast_dynamic-update-slice_fusion.5
  935.3 29.5 %custom-call.25 = f32[3,128,128]{1,2,0:T(8,128)S(1)} custom-call(f32[3,128,128]{2,1,0:T(8,128)S(1)} %pad_maximum_fusion.1), custom_call_target="InvertDiagBlocksLowerTriangular" | custom-call | tf_op jit(solution)/shard_map/triangular_solve/custom-call.2 | solution.py:15
  969.8 113.0 %all-reduce.18.cloned.1.call-done = f32[1,320,320]{1,0,2:T(1,128)} async-done(((f32[1,320,320]{1,0,2:T(1,128)}), f32[1,320,320]{1,0,2:T(1,128)}) %all-reduce.18.cloned.1.call-update) | async-done | bytes 409616
  (99 shorter events, 26.5 us)
Async XLA Ops:
  6.5 552.8 %copy-start = (f32[320,320]{1,0:T(8,128)S(1)}, f32[320,320]{1,0:T(8,128)}, u32[]{:S(2)}) copy-start(f32[320,320]{1,0:T(8,128)} %param.12) | copy-start | bytes 1228804
  6.5 78.6 %copy-start.4 = (s32[2]{0:T(128)S(1)}, s32[2]{0:T(128)}, u32[]{:S(2)}) copy-start(s32[2]{0:T(128)} %param.14) | copy-start | bytes 28
  6.5 73.7 %all-gather.3.cloned.1.call-start = ((), (), s32[]{:S(2)}) async-start(), calls=%async_computation.1 | async-start | bytes 2785280 | tf_op jit(solution)/shard_map/all_gather | solution.py:29
  7.3 275.2 %all-reduce.10.cloned.1.call-start = ((), (), s32[]{:S(2)}) async-start(), calls=%async_computation.2 | async-start | bytes 327680 | tf_op jit(solution)/shard_map/psum | solution.py:36
  85.1 313.7 %all-reduce.12.cloned.1.call-start = ((), (), s32[]{:S(2)}) async-start(), calls=%async_computation.3 | async-start | bytes 983040 | tf_op jit(solution)/shard_map/psum | solution.py:19
  284.8 270.6 %all-gather.5.cloned.1.call-start = ((), (), s32[]{:S(2)}) async-start(), calls=%async_computation.4 | async-start | bytes 2785280 | tf_op jit(solution)/shard_map/all_gather | solution.py:38
  401.1 87.3 %copy-start.2 = (f32[128,320]{0,1:T(8,128)S(1)}, f32[128,320]{0,1:T(8,128)}, u32[]{:S(2)}) copy-start(f32[128,320]{0,1:T(8,128)} %all-reduce.10.cloned.1.call-done) | copy-start | bytes 491524
  423.0 67.6 %copy-start.1 = (f32[1,128,2048]{2,1,0:T(8,128)S(1)}, f32[1,128,2048]{2,1,0:T(8,128)}, u32[]{:S(2)}) copy-start(f32[1,128,2048]{2,1,0:T(8,128)} %param.9) | copy-start | bytes 3145732
  489.0 7.4 copy-start.5
  492.4 18.5 %all-to-all-start = ((f32[1,128,2048]{1,0,2:T(1,128)}), f32[1,128,2048]{1,0,2:T(1,128)S(1)}, u32[]{:S(2)}, u32[]{:S(2)}) async-start(f32[1,128,2048]{1,0,2:T(1,128)} %copy.29), calls=%async_computation | async-start | bytes 2097152 | tf_op jit(solution)/shard_map/all_to_all | solution.py:25
  496.3 262.2 %all-reduce.14.cloned.1.call-start = ((), (), s32[]{:S(2)}) async-start(), calls=%async_computation.5 | async-start | bytes 327680 | tf_op jit(solution)/shard_map/psum | solution.py:52
  561.1 313.5 %all-reduce.16.cloned.1.call-start = ((), (), s32[]{:S(2)}) async-start(), calls=%async_computation.6 | async-start | bytes 983040 | tf_op jit(solution)/shard_map/psum | solution.py:19
  760.8 322.0 %all-reduce.18.cloned.1.call-start = ((), (), s32[]{:S(2)}) async-start(), calls=%async_computation.7 | async-start | bytes 983040
  876.9 87.9 %copy-start.3 = (f32[128,320]{0,1:T(8,128)S(1)}, f32[128,320]{0,1:T(8,128)}, u32[]{:S(2)}) copy-start(f32[128,320]{0,1:T(8,128)} %all-reduce.14.cloned.1.call-done) | copy-start | bytes 491524
Sparse Core Ops, SparseCore 0:
  10.3 69.8 all-gather.2
  85.2 197.2 all-reduce.9
  286.1 112.6 all-reduce.11
  490.6 64.6 all-gather.4
  561.2 197.2 all-reduce.13
  761.9 112.6 all-reduce.15
  968.0 114.7 all-reduce.17
where the time goes:
time: 1090 us
  waiting for transfers between devices  865 us (79%)
  other arithmetic  166 us (15%)
  matrix products  20 us (2%)
  between operations  18.6 us (2%)
  local copies, waits for them, and re-layouts  17.4 us (2%)
    psum x2, waiting for transfers between devices, orthonormal(): return cholesky_pass(block, lax.psum(gram_of(block), 'row'))  226 us
    psum x1, waiting for transfers between devices, local(): sketch_two = lax.psum(local_two, 'fiber')  197 us
    psum x1, waiting for transfers between devices, local(): sketch_one = lax.psum(local_one, 'fiber')  197 us
    unnamed x8, waiting for transfers between devices  114 us
    another operation x21, other arithmetic, cholesky_pass(): lower = jnp.linalg.cholesky(gram)  102 us
    all_gather x1, waiting for transfers between devices, local(): lax.all_gather(row_sketch, 'row', axis=0, tiled=True)  72.2 us
    another operation x11, other arithmetic, cholesky_pass(): lax.linalg.triangular_solve(lower, block, left_side=False, lower=True, tr...  59.3 us
    all_gather x1, waiting for transfers between devices, local(): full_basis = lax.all_gather(kept_one, 'row', axis=0, tiled=True)  44.2 us
  transfers between devices with their start and end apart: 8, of which 8 were waited for; matrix products, arithmetic and copies ran while one was open for 1% of the time, Pallas kernels for 0%

commit v1 on v0

v1 whole, which is shorter than its diff:
```python
import jax
import jax.numpy as jnp
from jax import lax
from jax.experimental import pallas as pl
from jax.experimental.pallas import tpu as pltpu
from jax.sharding import PartitionSpec as P

F32, BF16 = jnp.float32, jnp.bfloat16
MESH = pl.DeviceIdType.MESH
S, HALF, SUB, BLOCK = 320, 160, 80, 64
SIDE = 4
ROWS = SIDE * SIDE
CHIPS = 16
LANES = 128


def split(value):
    high = value.astype(BF16)
    return high, (value - high.astype(F32)).astype(BF16)


def dot3(left, right, contract):
    numbers = ((contract[:1], contract[1:]), ((), ()))

    def one(a, b):
        return lax.dot_general(a, b, numbers, preferred_element_type=F32)

    (ah, al), (bh, bl) = left, right
    return one(ah, bh) + (one(ah, bl) + one(al, bh))


def factor_block(rows):
    sub = lax.broadcasted_iota(jnp.int32, (8, LANES), 0)
    wide = lambda piece: jnp.broadcast_to(piece, (8, LANES))
    rows, outs = list(rows), []
    for p in range(8):
        n = 8 - p
        col = [[wide(rows[p + v][:, 8 * p + k : 8 * p + k + 1]) for k in range(8)] for v in range(n)]
        row = [wide(rows[p][k : k + 1, :]) for k in range(8)]
        a = {(i, k): wide(col[0][k][i : i + 1, :]) for k in range(8) for i in range(k, 8)}
        out = None
        for k in range(8):
            inverse = 1.0 / a[k, k]
            for j in range(k + 1, 8):
                for i in range(j, 8):
                    a[i, j] = a[i, j] - (a[i, k] * a[j, k]) * inverse
            for j in range(k + 1, 8):
                factor = a[j, k] * inverse
                row[j] = row[j] - factor * row[k]
                for v in range(1, n):
                    col[v][j] = col[v][j] - factor * col[v][k]
            scaled = row[k] * inverse
            for v in range(1, n):
                rows[p + v] = rows[p + v] - col[v][k] * scaled
            final = row[k] * lax.rsqrt(a[k, k])
            out = final if out is None else jnp.where(sub == k, final, out)
        outs.append(out)
    return outs


def cholesky_steps(first, last, g, x, done):
    lane = lax.broadcasted_iota(jnp.int32, (8, LANES), 1)
    sub = lax.broadcasted_iota(jnp.int32, (8, LANES), 0)
    width = x.shape[1]

    def step(index, carry):
        rows = [
            jnp.where(
                lane < BLOCK,
                g[8 * i : 8 * i + 8, :LANES],
                jnp.where(lane - BLOCK == sub + 8 * i, 1.0, 0.0),
            )
            for i in range(8)
        ]
        block = jnp.concatenate(factor_block(rows), axis=0)
        inverse = split(block[:, BLOCK:])
        upper = dot3(inverse, split(g[:BLOCK, :]), (1, 0))
        solved = dot3(inverse, split(x[:BLOCK, :]), (1, 0))
        done[pl.ds(pl.multiple_of(index * BLOCK, BLOCK), BLOCK), :] = solved
        rest = split(upper[:, BLOCK:S])
        rest_t = split(upper[:, BLOCK:S].T)
        g[: S - BLOCK, : S - BLOCK] = g[BLOCK:, BLOCK:S] - dot3(rest_t, rest, (1, 0))
        x[: S - BLOCK, :] = x[BLOCK:, :] - dot3(rest_t, split(solved), (1, 0))
        return carry

    lax.fori_loop(first, last, step, 0)


def kernel(
    d_ref, rs_ref, w_ref, cs_ref, w2_ref, ranks_ref, out_ref,
    d_sib, d_high, d_low, w_own, w_sib, rst, rst_high, rst_low, regrouped,
    chunks, parts, sums, ys, y_high, y_low, cs_high, cs_low, w2_col,
    g, xa, pc, mixed_in, mixed_out, xi, winv, bt_out, bt_in, bt_all, bt,
    sib_sem, gather_recv, gather_send, pass_sem, z_send, z_recv, re_send, re_recv, b_send, b_recv,
):
    fiber, me = lax.axis_index("fiber"), lax.axis_index("row")
    z, core = lax.div(fiber, 2), lax.rem(fiber, 2)
    x, y = lax.div(me, SIDE), lax.rem(me, SIDE)
    other = 1 - core
    sibling = (2 * z + other, me)

    def at(dx, dy):
        return lax.rem(x + dx + SIDE, SIDE) * SIDE + lax.rem(y + dy + SIDE, SIDE)

    def along(axis, distance):
        return at(distance, 0) if axis == 0 else at(0, distance)

    def z_peer(distance):
        return lax.rem(z + distance, CHIPS)

    def remote(src, dst, send, recv, device):
        copy = pltpu.make_async_remote_copy(
            src_ref=src, dst_ref=dst, send_sem=send, recv_sem=recv, device_id=device, device_id_type=MESH
        )
        copy.start()
        return copy

    def wait_bytes(ref, sem):
        pltpu.make_async_copy(ref, ref, sem).wait()

    peers = [sibling]
    peers += [(fiber, at(dx, dy)) for dx in range(SIDE) for dy in range(SIDE) if dx or dy]
    peers += [(2 * z_peer(e) + core, me) for e in range(1, CHIPS)]
    barrier = pltpu.get_barrier_semaphore()
    for peer in peers:
        pl.semaphore_signal(barrier, inc=1, device_id=peer, device_id_type=MESH)

    rs_t = rs_ref[...].T
    for c in range(2):

        @pl.when(core == c)
        def _():
            rst[me] = rs_t[c * HALF : (c + 1) * HALF]

    w_t = jnp.broadcast_to(w_ref[...], (LANES, S)).T
    w_own[0], w_own[1] = w_t[:HALF], w_t[HALF:]
    pl.semaphore_wait(barrier, len(peers))

    def gather(buf, which, forward=None):
        send = gather_send.at[which]

        def recv(s, j, kind):
            return gather_recv.at[which, s, j, kind]

        def push(s, slot, axis, sign, part, j, kind):
            start, size = (s * SUB, SUB) if part is None else (s * SUB + part * (SUB // 2), SUB // 2)
            ref = buf(slot, start, size)
            remote(ref, ref, send, recv(s, j, kind), (fiber, along(axis, sign)))

        def arrived(s, slot, part, j, kind):
            start, size = (s * SUB, SUB) if part is None else (s * SUB + part * (SUB // 2), SUB // 2)
            wait_bytes(buf(slot, start, size), recv(s, j, kind))

        def place(s, i1, i2):
            return at(i1, i2) if s == 0 else at(i2, i1)

        offsets = (0, -1, 1, 2)

        def both(s, axis, slot, j):
            push(s, slot, axis, 1, None, j, 0)
            push(s, slot, axis, -1, None, j, 1)

        def done(s, i1, i2):
            if forward is not None:
                forward(s, place(s, i1, i2))

        for s in range(2):
            both(s, s, place(s, 0, 0), 0)
        for s in range(2):
            both(s, 1 - s, place(s, 0, 0), 1)
        for s in range(2):
            done(s, 0, 0)
        for kind, sign in ((0, 1), (1, -1)):
            for s in range(2):
                slot = place(s, -sign, 0)
                arrived(s, slot, None, 0, kind)
                push(s, slot, s, sign, kind, 0, 2 + kind)
                both(s, 1 - s, slot, 2 + kind)
                done(s, -sign, 0)
        for kind, sign in ((0, 1), (1, -1)):
            for s in range(2):
                slot = place(s, 0, -sign)
                arrived(s, slot, None, 1, kind)
                push(s, slot, 1 - s, sign, kind, 1, 2 + kind)
                done(s, 0, -sign)
        for s in range(2):
            slot = place(s, 2, 0)
            for kind in range(2):
                arrived(s, slot, kind, 0, 2 + kind)
            both(s, 1 - s, slot, 4)
            done(s, 2, 0)
        for j in (2, 3, 4):
            for kind, sign in ((0, 1), (1, -1)):
                for s in range(2):
                    slot = place(s, offsets[j - 1], -sign)
                    arrived(s, slot, None, j, kind)
                    push(s, slot, 1 - s, sign, kind, j, 2 + kind)
                    done(s, offsets[j - 1], -sign)
        for j in (1, 2, 3, 4):
            for s in range(2):
                slot = place(s, offsets[j - 1], 2)
                for kind in range(2):
                    arrived(s, slot, kind, j, 2 + kind)
                done(s, offsets[j - 1], 2)

    def fiber_sum(value, which):
        for i in range(CHIPS):
            chunks[which, i] = value[10 * i : 10 * i + 10]
        sent, got = z_send.at[which], z_recv.at[which]
        for e in range(1, CHIPS):
            to = z_peer(e)
            remote(chunks.at[which, to], parts.at[which, z], sent.at[0], got.at[0], (2 * to + core, me))
        parts[which, z] = chunks[which, z]
        wait_bytes(parts.at[which, pl.ds(0, CHIPS - 1)], got.at[0])
        total = parts[which, 0]
        for i in range(1, CHIPS):
            total = total + parts[which, i]
        sums[which, z] = total
        for e in range(1, CHIPS):
            to = z_peer(e)
            remote(sums.at[which, z], sums.at[which, z], sent.at[1], got.at[1], (2 * to + core, me))
        wait_bytes(sums.at[which, pl.ds(0, CHIPS - 1)], got.at[1])
        return jnp.concatenate([sums[which, i] for i in range(CHIPS)], axis=0)

    to_sibling = [
        remote(d_ref.at[0], d_sib, sib_sem.at[0, 0], sib_sem.at[1, 0], sibling),
        remote(w_own.at[other], w_sib, sib_sem.at[0, 1], sib_sem.at[1, 1], sibling),
    ]
    gather(lambda slot, start, size: rst.at[slot, pl.ds(start, size)], 0)
    for dx in range(SIDE):
        for dy in range(SIDE):
            if dx or dy:
                to = at(dx, dy)
                remote(
                    d_ref.at[0, :, pl.ds(pl.multiple_of(to * LANES, LANES), LANES)],
                    regrouped.at[me], re_send, re_recv, (fiber, to),
                )
    cs_high[...], cs_low[...] = split(cs_ref[...].T)
    w2_col[...] = jnp.broadcast_to(w2_ref[...], (LANES, S)).T
    d_high[:LANES], d_low[:LANES] = split(d_ref[0])
    for j in range(ROWS):
        rst_high[:, j * LANES : (j + 1) * LANES], rst_low[:, j * LANES : (j + 1) * LANES] = split(rst[j])
    regrouped[me] = d_ref[0, :, pl.ds(pl.multiple_of(me * LANES, LANES), LANES)]
    for copy in to_sibling:
        copy.wait_recv()
    d_high[LANES:], d_low[LANES:] = split(d_sib[...])
    both_slabs = dot3((rst_high[...], rst_low[...]), (d_high[...], d_low[...]), (1, 1))
    one = fiber_sum(both_slabs[:, :LANES] * w_own[core] + both_slabs[:, LANES:] * w_sib[...], 0)

    def gather_sketch(which, value):
        buf = ys.at[which]
        buf[me, core] = value

        def forward(s, slot):
            ref = buf.at[slot, core, pl.ds(s * SUB, SUB)]
            remote(ref, ref, pass_sem.at[0, which], pass_sem.at[1, which], sibling)

        gather(lambda slot, start, size: buf.at[slot, core, pl.ds(start, size)], 1 + which, forward)
        wait_bytes(buf.at[:, other], pass_sem.at[1, which])
        for j in range(ROWS):
            block = buf[j].reshape(S, LANES)
            y_high[:, j * LANES : (j + 1) * LANES], y_low[:, j * LANES : (j + 1) * LANES] = split(block)
        pair = (y_high[...], y_low[...])
        g[...] = dot3(pair, pair, (1, 1))
        return pair

    pair = gather_sketch(0, one)
    wait_bytes(regrouped.at[pl.ds(0, ROWS - 1)], re_recv)
    xa[...] = dot3(pair, split(regrouped[...].reshape(ROWS * LANES, LANES)), (1, 0))
    cholesky_steps(0, S // BLOCK, g, xa, pc)
    index = lax.broadcasted_iota(jnp.int32, (S, LANES), 0)
    pc[...] = jnp.where(index < ranks_ref[0], pc[...], 0.0)

    pc_pair = split(pc[...])
    mixed = dot3((cs_high[...], cs_low[...]), pc_pair, (1, 0)) * w2_col[...]
    mixed_out[0], mixed_out[1] = mixed[:HALF], mixed[HALF:]
    exchange = remote(mixed_out.at[other], mixed_in, sib_sem.at[0, 2], sib_sem.at[1, 2], sibling)
    exchange.wait_recv()
    to_sibling.append(exchange)
    gather_sketch(1, fiber_sum(mixed_out[core] + mixed_in[...], 1))

    local_two = split(ys[1, me].reshape(S, LANES))
    bt_part = dot3(local_two, pc_pair, (1, 1))
    for j in range(ROWS):
        bt_out[j] = bt_part[20 * j : 20 * j + 20]
    for dx in range(SIDE):
        for dy in range(SIDE):
            if dx or dy:
                to = at(dx, dy)
                remote(bt_out.at[to], bt_in.at[me], b_send.at[0], b_recv.at[0], (fiber, to))
    bt_in[me] = bt_out[me]
    square = (S, S)
    xi[...] = jnp.where(
        lax.broadcasted_iota(jnp.int32, square, 0) == lax.broadcasted_iota(jnp.int32, square, 1), 1.0, 0.0
    )
    cholesky_steps(0, 2, g, xi, winv)
    wait_bytes(bt_in.at[pl.ds(0, ROWS - 1)], b_recv.at[0])
    total = bt_in[0]
    for j in range(1, ROWS):
        total = total + bt_in[j]
    bt_all[me] = total
    for dx in range(SIDE):
        for dy in range(SIDE):
            if dx or dy:
                to = at(dx, dy)
                remote(bt_all.at[me], bt_all.at[me], b_send.at[1], b_recv.at[1], (fiber, to))
    cholesky_steps(2, S // BLOCK, g, xi, winv)
    wait_bytes(bt_all.at[pl.ds(0, ROWS - 1)], b_recv.at[1])
    for j in range(ROWS):
        bt[20 * j : 20 * j + 20, :] = bt_all[j]
        bt_out_row = winv[20 * j : 20 * j + 20, :]
        bt_in[j] = bt_out_row
    mine = bt_in[me]
    keep = lax.broadcasted_iota(jnp.int32, mine.shape, 0) + 20 * me < ranks_ref[1]
    mine = jnp.where(keep, mine, 0.0)
    core_t = dot3(split(mine), split(bt[...]), (1, 0))
    out_ref[0] = core_t.T

    for copy in to_sibling:
        copy.wait_send()
    for which in range(3):
        wait_bytes(rst.at[pl.ds(0, ROWS - 1)], gather_send.at[which])
    for which in range(2):
        wait_bytes(ys.at[which, :, core], pass_sem.at[0, which])
        for i in range(2):
            wait_bytes(parts.at[which, pl.ds(0, CHIPS - 1)], z_send.at[which, i])
    wait_bytes(regrouped.at[pl.ds(0, ROWS - 1)], re_send)
    for i in range(2):
        wait_bytes(bt_in.at[pl.ds(0, ROWS - 1)], b_send.at[i])


def local(deltas, row_sketch, slab_sketch, core_sketch, slab_sketch_two, ranks):
    vmem = lambda *shape: pltpu.VMEM(shape, F32)
    half = lambda *shape: pltpu.VMEM(shape, BF16)
    dma = pltpu.SemaphoreType.DMA
    in_vmem = pl.BlockSpec(memory_space=pltpu.VMEM)
    return pl.pallas_call(
        kernel,
        out_shape=jax.ShapeDtypeStruct((1, S, S // ROWS), F32),
        in_specs=[in_vmem] * 5 + [pl.BlockSpec(memory_space=pltpu.SMEM)],
        out_specs=in_vmem,
        scratch_shapes=[
            vmem(LANES, 2048),
            half(2 * LANES, 2048), half(2 * LANES, 2048),
            vmem(2, HALF, LANES), vmem(HALF, LANES),
            vmem(ROWS, HALF, LANES), half(HALF, 2048), half(HALF, 2048),
            vmem(ROWS, LANES, LANES),
            vmem(2, CHIPS, 10, LANES), vmem(2, CHIPS, 10, LANES), vmem(2, CHIPS, 10, LANES),
            vmem(2, ROWS, 2, HALF, LANES),
            half(S, 2048), half(S, 2048),
            half(S, S), half(S, S), vmem(S, LANES),
            vmem(S, S), vmem(S, LANES), vmem(S, LANES),
            vmem(HALF, LANES), vmem(2, HALF, LANES),
            vmem(S, S), vmem(S, S),
            vmem(ROWS, 20, S), vmem(ROWS, 20, S), vmem(ROWS, 20, S), vmem(S, S),
            dma((2, 3)),
            dma((3, 2, 5, 4)), dma((3,)),
            dma((2, 2)),
            dma((2, 2)), dma((2, 2)),
            dma(()), dma(()),
            dma((2,)), dma((2,)),
        ],
        compiler_params=pltpu.CompilerParams(
            collective_id=0, has_side_effects=True, vmem_limit_bytes=48 * 2**20
        ),
        cost_estimate=pl.CostEstimate(flops=2 * 10**9, bytes_accessed=4 * 10**6, transcendentals=0),
    )(deltas, row_sketch, slab_sketch, core_sketch, slab_sketch_two, ranks)


def solution(mesh):
    in_specs = (
        P("fiber", "row", None),
        P("row", None),
        P("fiber", None),
        P(),
        P("fiber", None),
        P(),
    )
    out_specs = P("fiber", None, "row")
    return jax.shard_map(local, mesh=mesh, in_specs=in_specs, out_specs=out_specs, check_vma=False)
```

time: 1090 us -> 152 us (0.14)
  waiting for transfers between devices: 865 us -> 0 us
  other arithmetic: 166 us -> 0 us
  Pallas kernels: 0 us -> 147 us
  matrix products: 20 us -> 0 us
  between operations: 18.6 us -> 0.05 us
  local copies, waits for them, and re-layouts: 17.4 us -> 4.06 us
    psum x4 -> x0, waiting for transfers between devices: 620 us -> none  [the longest x2 226 us: orthonormal(): return cholesky_pass(block, lax.psum(gram_of(block), 'row'))]
    another operation x32 -> x0, other arithmetic: 161 us -> none  [the longest x21 102 us: cholesky_pass(): lower = jnp.linalg.cholesky(gram)]
    pallas_call x0 -> x1, Pallas kernels: none -> 147 us  [local(): pl.pallas_call(kernel, out_shape=jax.ShapeDtypeStruct((1, S, S // ROWS),...]
    all_gather x2 -> x0, waiting for transfers between devices: 116 us -> none  [the longest x1 72.2 us: local(): lax.all_gather(row_sketch, 'row', axis=0, tiled=True)]
    unnamed x8 -> x0, waiting for transfers between devices: 114 us -> none
    dot_general x6 -> x0, matrix products: 15.8 us -> none  [the longest x1 4.86 us: local(): jnp.einsum('mpq,qs->mps', deltas, lax.all_gather(row_sketch, 'row', axis=...]
    all_to_all x1 -> x0, waiting for transfers between devices: 14.6 us -> none  [local(): lax.all_to_all(deltas, 'row', split_axis=2, concat_axis=1, tiled=True)]
  transfers between devices with their start and end apart: 8 -> 0, of which waited for: 8 -> 0; matrix products, arithmetic and copies ran while one was open for 1% -> 0% of each run, Pallas kernels for 0% -> 0%
where the time goes in v1:
time: 152 us
  Pallas kernels  147 us (97%)
  local copies, waits for them, and re-layouts  4.06 us (3%)
    pallas_call x1, Pallas kernels, local(): pl.pallas_call(kernel, out_shape=jax.ShapeDtypeStruct((1, S, S // ROWS),...  147 us
    unnamed x11, local copies, waits for them, and re-layouts  3.34 us

profile of v1, /device:TPU:1, one launch (start us, length us, event | category | flops | bytes accessed | tf_op | source)
XLA Modules:
  0.0 151.5 jit_solution(809685768225770594)
XLA Ops:
  0.0 0.0 copy-start.4
  0.0 0.0 copy-start.3
  0.0 0.0 copy-start.2
  0.0 1.1 copy.7.rs_ref
  1.1 0.0 copy-done.4
  1.1 0.0 copy-done.3
  1.1 0.0 copy-done.2
  1.1 0.0 copy-start
  1.1 1.2 copy-done
  2.4 0.0 copy-start.1
  2.4 1.0 copy-done.1
  3.4 147.4 %shard_map.64 = f32[1,320,20]{2,1,0:T(8,128)S(1)} custom-call(f32[1,128,2048]{2,1,0:T(8,128)S(1)} %copy-done, f32[128,320]{1,0:T(8,128)S(1)} %copy.7.rs_ref, f32[1,320]{1,0:T(1,128)S(1)} %copy-done.2, f32[320,320]{1,0:T(8,128)S(1)} %copy-done.1, f32[1,320]{1,0:T(1,128)S(1)} %copy-done.3, s32[2]{0:T(128)S(1)} %copy-done.4), custom_call_target="tpu_custom_call" | custom-call | flops 2000000000 | bytes 4000000 | tf_op jit(solution)/shard_map/pallas_call | solution.py:337
  150.8 0.7 copy.8
Async XLA Ops:
  0.0 1.1 copy-start.4
  0.0 1.1 copy-start.3
  0.0 1.1 copy-start.2
  1.1 1.2 copy-start
  2.4 1.0 copy-start.1

commit v2 on v0

v2 whole, which is shorter than its diff:
```python
import jax
import jax.numpy as jnp
from jax import lax
from jax.experimental import pallas as pl
from jax.experimental.pallas import tpu as pltpu
from jax.sharding import PartitionSpec as P

F32, BF16 = jnp.float32, jnp.bfloat16
MESH = pl.DeviceIdType.MESH
S, HALF, SUB, BLOCK = 320, 160, 80, 64
SIDE = 4
ROWS = SIDE * SIDE
CHIPS = 16
LANES = 128
CROSS = [(0, 0), (1, 0), (3, 0), (0, 1), (0, 3), (2, 0), (0, 2)]
DIAGONAL = [(1, 1), (1, 3), (3, 1), (3, 3)]
FAR = [(1, 2), (3, 2), (2, 1), (2, 3), (2, 2)]
GROUPS = [CROSS, DIAGONAL, FAR]
OTHERS = [offset for group in GROUPS[::-1] for offset in group[::-1] if offset != (0, 0)]
AWAY = [8, 7, 9, 6, 10, 5, 11, 4, 12, 3, 13, 2, 14, 1, 15]


def split(value):
    high = value.astype(BF16)
    return high, (value - high.astype(F32)).astype(BF16)


def dot3(left, right, contract):
    numbers = ((contract[:1], contract[1:]), ((), ()))

    def one(a, b):
        return lax.dot_general(a, b, numbers, preferred_element_type=F32)

    (ah, al), (bh, bl) = left, right
    return one(ah, bh) + (one(ah, bl) + one(al, bh))


def stack3(left, right, contract):
    (ah, al), (bh, bl) = left, right
    return lax.dot_general(
        jnp.concatenate([ah, ah, al], axis=contract[0]),
        jnp.concatenate([bh, bl, bh], axis=contract[1]),
        (((contract[0],), (contract[1],)), ((), ())),
        preferred_element_type=F32,
    )


def factor_block(rows):
    sub = lax.broadcasted_iota(jnp.int32, (8, LANES), 0)

    def wide(piece):
        return jnp.broadcast_to(piece, (8, LANES))

    def lane_of(array, lane):
        return jnp.take_along_axis(array, jnp.full((8, LANES), lane, jnp.int32), axis=1)

    rows, outs = list(rows), []
    for p in range(8):
        row = [wide(rows[p][k : k + 1, :]) for k in range(8)]
        own = [lane_of(rows[p], 8 * p + k) for k in range(8)]
        a = {(i, k): wide(own[k][i : i + 1, :]) for k in range(8) for i in range(k, 8)}
        col = [lane_of(rows[p + 1], 8 * p + k) for k in range(8)] if p < 7 else None
        out = None
        for k in range(8):
            inverse = 1.0 / a[k, k]
            for j in range(k + 1, 8):
                factor = a[j, k] * inverse
                for i in range(j, 8):
                    a[i, j] = a[i, j] - a[i, k] * factor
                row[j] = row[j] - factor * row[k]
                if col:
                    col[j] = col[j] - factor * col[k]
            if col:
                rows[p + 1] = rows[p + 1] - col[k] * (row[k] * inverse)
            final = row[k] * lax.rsqrt(a[k, k])
            out = final if out is None else jnp.where(sub == k, final, out)
        outs.append(out)
        if p < 6:
            high = out.astype(BF16).astype(F32)
            low = out - high
            left = jnp.concatenate([high, high, low], axis=0)[:, :BLOCK].astype(BF16)
            right = jnp.concatenate([high, low, high], axis=0).astype(BF16)
            update = lax.dot_general(left, right, (((0,), (0,)), ((), ())), preferred_element_type=F32)
            for i in range(p + 2, 8):
                rows[i] = rows[i] - update[8 * i : 8 * i + 8]
    return outs


def cholesky_inverse(g, x, done, beside):
    lane = lax.broadcasted_iota(jnp.int32, (8, LANES), 1)
    sub = lax.broadcasted_iota(jnp.int32, (8, LANES), 0)

    def step(index, carry):
        beside(index)
        rows = [
            jnp.where(
                lane < BLOCK,
                g[8 * i : 8 * i + 8, :LANES],
                jnp.where(lane - BLOCK == sub + 8 * i, 1.0, 0.0),
            )
            for i in range(8)
        ]
        block = jnp.concatenate(factor_block(rows), axis=0)
        inverse = split(block[:, BLOCK:])
        upper = stack3(inverse, split(g[:BLOCK, :]), (1, 0))
        solved = stack3(inverse, split(x[:BLOCK, :]), (1, 0))
        done[pl.ds(pl.multiple_of(index * BLOCK, BLOCK), BLOCK), :] = solved
        rest = split(upper[:, BLOCK:])
        g[: S - BLOCK, : S - BLOCK] = g[BLOCK:, BLOCK:] - stack3(rest, rest, (0, 0))
        x[: S - BLOCK, :] = x[BLOCK:, :] - stack3(rest, split(solved), (0, 0))
        return carry

    lax.fori_loop(0, S // BLOCK, step, 0)


def kernel(
    d_hbm, rs_hbm, w_ref, cs_hbm, w2_ref, ranks_ref, out_ref,
    d_own, d_sib, d_high, d_low, w_own, w_sib, rst, rst_high, rst_low, regrouped, cs_ref,
    chunks, parts, sums, ys, y_high, y_low, cs_high, cs_low, w2_col,
    g, pc, mixed_in, mixed_out, xi, winv, bt_out, bt_in, bt_all, bt, first_sum,
    g_out, g_in, g_all, w_rows,
    in_sem, sib_sem, gather_recv, gather_send, pass_send, pass_recv,
    z_send, z_recv, re_send, re_recv, b_send, b_recv, own_sem, g_send, g_recv,
):
    fiber, me = lax.axis_index("fiber"), lax.axis_index("row")
    z, core = lax.div(fiber, 2), lax.rem(fiber, 2)
    x, y = lax.div(me, SIDE), lax.rem(me, SIDE)
    other = 1 - core
    sibling = (2 * z + other, me)
    closing = []

    def at(dx, dy):
        return lax.rem(x + dx + SIDE, SIDE) * SIDE + lax.rem(y + dy + SIDE, SIDE)

    def z_peer(distance):
        return lax.rem(z + distance, CHIPS)

    def remote(src, dst, send, recv, device):
        copy = pltpu.make_async_remote_copy(
            src_ref=src, dst_ref=dst, send_sem=send, recv_sem=recv, device_id=device, device_id_type=MESH
        )
        copy.start()
        return copy

    def wait_bytes(ref, sem):
        pltpu.make_async_copy(ref, ref, sem).wait()

    def fetch(src, dst, i):
        copy = pltpu.make_async_copy(src, dst, in_sem.at[i])
        copy.start()
        return copy

    half_of_core = pl.ds(pl.multiple_of(core * HALF, HALF), HALF)
    fetch_rs = fetch(rs_hbm.at[half_of_core], rst.at[me], 0)
    fetch_d = fetch(d_hbm.at[0], d_own, 1)
    fetch_cs = fetch(cs_hbm, cs_ref, 2)
    peers = [(2 * z_peer(e) + core, me) for e in AWAY]
    peers += [(fiber, at(dx, dy)) for dx, dy in OTHERS]
    peers += [(2 * z + other, at(dx, dy)) for dx, dy in OTHERS]
    peers += [sibling]
    barrier = pltpu.get_barrier_semaphore()
    for peer in peers:
        pl.semaphore_signal(barrier, inc=1, device_id=peer, device_id_type=MESH)
    w_t = jnp.broadcast_to(w_ref[...], (LANES, S)).T
    w_own[0], w_own[1] = w_t[:HALF], w_t[HALF:]
    fetch_rs.wait()
    fetch_d.wait()
    pl.semaphore_wait(barrier, len(peers))

    def gather(buf, which):
        send = gather_send.at[which]
        closing.append(lambda: wait_bytes(rst.at[pl.ds(0, ROWS - 1)], send))

        def piece(s, slot):
            return buf(slot, s * SUB, SUB)

        def push(s, slot, axis, j):
            for d in (2, 1, 3):
                ref = piece(s, slot)
                to = at(d, 0) if axis == 0 else at(0, d)
                remote(ref, ref, send, gather_recv.at[which, s, j, d - 1], (fiber, to))

        def arrived(s, ex, ey):
            near, last = (ex, ey) if s == 0 else (ey, ex)
            sem = gather_recv.at[which, s, 1 + near, last - 1] if last else gather_recv.at[which, s, 0, near - 1]
            slot = at(-ex, -ey)
            wait_bytes(piece(s, slot), sem)
            if not last:
                push(s, slot, 1 - s, 1 + near)

        def start():
            for s in range(2):
                push(s, me, s, 0)
            for s in range(2):
                push(s, me, 1 - s, 1)

        def first():
            for e in (1, 3, 2):
                for s in range(2):
                    arrived(s, *((e, 0) if s == 0 else (0, e)))

        def rest(offsets):
            for ex, ey in offsets:
                for s in range(2):
                    if (ex, ey)[1 - s]:
                        arrived(s, ex, ey)

        return start, first, rest

    def add_to(ref, first, value):
        ref[...] = value if first == 0 else ref[...] + value

    def fiber_sum(value, which):
        for i in range(CHIPS):
            chunks[which, i] = value[10 * i : 10 * i + 10]
        sent, got = z_send.at[which], z_recv.at[which]
        for i in range(2):
            closing.append(lambda i=i: wait_bytes(parts.at[which, pl.ds(0, CHIPS - 1)], sent.at[i]))
        for e in AWAY:
            to = z_peer(e)
            remote(chunks.at[which, to], parts.at[which, z], sent.at[0], got.at[0], (2 * to + core, me))
        parts[which, z] = chunks[which, z]
        wait_bytes(parts.at[which, pl.ds(0, CHIPS - 1)], got.at[0])
        total = parts[which, 0]
        for i in range(1, CHIPS):
            total = total + parts[which, i]
        sums[which, z] = total
        for e in AWAY:
            to = z_peer(e)
            remote(sums.at[which, z], sums.at[which, z], sent.at[1], got.at[1], (2 * to + core, me))
        wait_bytes(sums.at[which, pl.ds(0, CHIPS - 1)], got.at[1])
        return jnp.concatenate([sums[which, i] for i in range(CHIPS)], axis=0)

    to_sibling = [
        remote(d_own, d_sib, sib_sem.at[0, 0], sib_sem.at[1, 0], sibling),
        remote(w_own.at[other], w_sib, sib_sem.at[0, 1], sib_sem.at[1, 1], sibling),
    ]
    for copy in to_sibling:
        closing.append(copy.wait_send)

    def columns(slot):
        return pl.ds(pl.multiple_of(slot * LANES, LANES), LANES)

    def first_group(first, slots):
        if first == 0:
            fetch_cs.wait()
            cs_high[...], cs_low[...] = split(cs_ref[...].T)
            w2_col[...] = jnp.broadcast_to(w2_ref[...], (LANES, S)).T
            for copy in to_sibling:
                copy.wait_recv()
            i = 0
            for offsets in GROUPS:
                for ex, ey in offsets:
                    cols = columns(at(-ex, -ey))
                    here = slice(i * LANES, (i + 1) * LANES)
                    d_high[:LANES, here], d_low[:LANES, here] = split(d_own[:, cols])
                    d_high[LANES:, here], d_low[LANES:, here] = split(d_sib[:, cols])
                    i += 1
        if first + len(slots) == ROWS:
            for dx, dy in OTHERS:
                to = at(dx, dy)
                remote(d_own.at[:, columns(to)], regrouped.at[me], re_send, re_recv, (fiber, to))
            closing.append(lambda: wait_bytes(regrouped.at[pl.ds(0, ROWS - 1)], re_send))
        for i, slot in enumerate(slots):
            here = slice((first + i) * LANES, (first + i + 1) * LANES)
            rst_high[:, here], rst_low[:, here] = split(rst[slot])
        here = slice(first * LANES, (first + len(slots)) * LANES)
        add_to(
            first_sum, first, dot3((rst_high[:, here], rst_low[:, here]), (d_high[:, here], d_low[:, here]), (1, 1))
        )

    start, first, rest = gather(lambda slot, start, size: rst.at[slot, pl.ds(start, size)], 0)
    start()
    first()
    count = 0
    for offsets in GROUPS:
        rest(offsets)
        first_group(count, [at(-ex, -ey) for ex, ey in offsets])
        count += len(offsets)
    regrouped[me] = d_own[:, columns(me)]
    one = fiber_sum(first_sum[:, :LANES] * w_own[core] + first_sum[:, LANES:] * w_sib[...], 0)

    def to_pair(value, which):
        ys[which, me, core] = value
        ref = ys.at[which, me, core]
        copy = remote(ref, ref, own_sem.at[0, which], own_sem.at[1, which], sibling)
        closing.append(copy.wait_send)
        copy.wait_recv()
        return ys[which, me].reshape(S, LANES)

    def gram_sum(block, which, beside):
        high, low = split(jnp.concatenate([block, jnp.zeros((LANES // 2, LANES), F32)], axis=0))
        for c, first in ((0, 0), (1, LANES)):

            @pl.when(core == c)
            def _():
                last = LANES if c == 0 else 3 * LANES
                part = stack3((high[first:last], low[first:last]), (high[first:], low[first:]), (1, 1))
                for i in range(ROWS):
                    strip = part[8 * i : 8 * i + 8]
                    if c == 0:
                        tiles = [strip[:, LANES * t : LANES * (t + 1)] for t in range(3)]
                    else:
                        tiles = [strip[:, :LANES], strip[:, LANES:], part[LANES + 8 * i : LANES + 8 * i + 8, LANES:]]
                    for t in range(3):
                        g_out[which, i, t] = tiles[t]

        for dx, dy in OTHERS:
            to = at(dx, dy)
            remote(g_out.at[which, to], g_in.at[which, me], g_send.at[which, 0], g_recv.at[which, 0], (fiber, to))
        g_in[which, me] = g_out[which, me]
        beside[0]()
        wait_bytes(g_in.at[which, pl.ds(0, ROWS - 1)], g_recv.at[which, 0])
        total = g_in[which, 0]
        for i in range(1, ROWS):
            total = total + g_in[which, i]
        g_all[which, core, me] = total
        ref = g_all.at[which, core, me]
        for dx, dy in OTHERS:
            to = at(dx, dy)
            remote(ref, ref, g_send.at[which, 1], g_recv.at[which, 1], (fiber, to))
            remote(ref, ref, g_send.at[which, 2], g_recv.at[which, 2], (2 * z + other, to))
        remote(ref, ref, g_send.at[which, 2], g_recv.at[which, 2], sibling)
        for i in range(2):
            closing.append(lambda i=i: wait_bytes(g_in.at[which, pl.ds(0, ROWS - 1)], g_send.at[which, i]))
        closing.append(lambda: wait_bytes(g_in.at[which], g_send.at[which, 2]))
        beside[1]()
        wait_bytes(g_all.at[which, core, pl.ds(0, ROWS - 1)], g_recv.at[which, 1])
        wait_bytes(g_all.at[which, other], g_recv.at[which, 2])
        for i in range(ROWS):
            strip, under = slice(8 * i, 8 * i + 8), slice(LANES + 8 * i, LANES + 8 * i + 8)
            g[strip, :LANES] = g_all[which, 0, i, 0]
            g[strip, LANES : 2 * LANES] = g_all[which, 0, i, 1]
            g[strip, 2 * LANES :] = g_all[which, 0, i, 2][:, : LANES // 2]
            g[under, LANES : 2 * LANES] = g_all[which, 1, i, 0]
            g[under, 2 * LANES :] = g_all[which, 1, i, 1][:, : LANES // 2]
            if i < ROWS // 2:
                g[2 * LANES + 8 * i : 2 * LANES + 8 * i + 8, 2 * LANES :] = g_all[which, 1, i, 2][:, : LANES // 2]

    square = (S, S)
    identity = jnp.where(
        lax.broadcasted_iota(jnp.int32, square, 0) == lax.broadcasted_iota(jnp.int32, square, 1), 1.0, 0.0
    )
    g[...] = identity
    xi[0], xi[1] = identity, identity
    buf = ys.at[0]
    block_one = to_pair(one, 0)
    start, first, rest = gather(lambda slot, start, size: buf.at[slot, core, pl.ds(start, size)], 1)
    gram_sum(block_one, 0, (start, first))

    def pass_on(index):
        @pl.when(index == 3)
        def _():
            for offsets in GROUPS:
                rest(offsets)
            for dx, dy in OTHERS:
                ref = buf.at[at(dx, dy), core]
                remote(ref, ref, pass_send, pass_recv, sibling)

    cholesky_inverse(g, xi.at[0], winv, pass_on)
    closing.append(lambda: wait_bytes(buf.at[pl.ds(0, ROWS - 1), core], pass_send))
    wait_bytes(buf.at[pl.ds(0, ROWS - 1), other], pass_recv)
    wait_bytes(regrouped.at[pl.ds(0, ROWS - 1)], re_recv)
    for j in range(ROWS):
        here = slice(j * LANES, (j + 1) * LANES)
        y_high[:, here], y_low[:, here] = split(buf[j].reshape(S, LANES))
    slabs = split(regrouped[...].reshape(ROWS * LANES, LANES))
    projected = dot3((y_high[...], y_low[...]), slabs, (1, 0))
    index = lax.broadcasted_iota(jnp.int32, (S, LANES), 0)
    pc[...] = jnp.where(index < ranks_ref[0], dot3(split(winv[...]), split(projected), (1, 0)), 0.0)

    pc_pair = split(pc[...])
    mixed = dot3((cs_high[...], cs_low[...]), pc_pair, (1, 0)) * w2_col[...]
    mixed_out[0], mixed_out[1] = mixed[:HALF], mixed[HALF:]
    exchange = remote(mixed_out.at[other], mixed_in, sib_sem.at[0, 2], sib_sem.at[1, 2], sibling)
    closing.append(exchange.wait_send)
    exchange.wait_recv()
    block_two = to_pair(fiber_sum(mixed_out[core] + mixed_in[...], 1), 1)

    def nothing():
        pass

    def project_two():
        bt_part = dot3(split(block_two), pc_pair, (1, 1))
        for j in range(ROWS):
            bt_out[j] = bt_part[20 * j : 20 * j + 20]

    gram_sum(block_two, 1, (nothing, project_two))
    for dx, dy in OTHERS:
        to = at(dx, dy)
        remote(bt_out.at[to], bt_in.at[me], b_send.at[0], b_recv.at[0], (fiber, to))
    bt_in[me] = bt_out[me]

    def add_up(index):
        @pl.when(index == 2)
        def _():
            wait_bytes(bt_in.at[pl.ds(0, ROWS - 1)], b_recv.at[0])
            total = bt_in[0]
            for j in range(1, ROWS):
                total = total + bt_in[j]
            bt_all[me] = total
            for dx, dy in OTHERS:
                to = at(dx, dy)
                remote(bt_all.at[me], bt_all.at[me], b_send.at[1], b_recv.at[1], (fiber, to))
            for close in closing:
                close()

    cholesky_inverse(g, xi.at[1], winv, add_up)
    wait_bytes(bt_all.at[pl.ds(0, ROWS - 1)], b_recv.at[1])
    for j in range(ROWS):
        bt[20 * j : 20 * j + 20, :] = bt_all[j]
        w_rows[j] = winv[20 * j : 20 * j + 20, :]
    mine = w_rows[me]
    keep = lax.broadcasted_iota(jnp.int32, mine.shape, 0) + 20 * me < ranks_ref[1]
    mine = jnp.where(keep, mine, 0.0)
    core_t = dot3(split(mine), split(bt[...]), (1, 0))
    for i in range(S // ROWS):
        out_ref[i] = core_t[i : i + 1]
    for i in range(2):
        wait_bytes(bt_all.at[pl.ds(0, ROWS - 1)], b_send.at[i])


def local(deltas, row_sketch, slab_sketch, core_sketch, slab_sketch_two, ranks):
    vmem = lambda *shape: pltpu.VMEM(shape, F32)
    half = lambda *shape: pltpu.VMEM(shape, BF16)
    dma = pltpu.SemaphoreType.DMA
    in_vmem = pl.BlockSpec(memory_space=pltpu.VMEM)
    in_hbm = pl.BlockSpec(memory_space=pltpu.HBM)
    core_t = pl.pallas_call(
        kernel,
        out_shape=jax.ShapeDtypeStruct((S // ROWS, 1, S), F32),
        in_specs=[in_hbm, in_hbm, in_vmem, in_hbm, in_vmem, pl.BlockSpec(memory_space=pltpu.SMEM)],
        out_specs=in_vmem,
        scratch_shapes=[
            vmem(LANES, 2048), vmem(LANES, 2048),
            half(2 * LANES, 2048), half(2 * LANES, 2048),
            vmem(2, HALF, LANES), vmem(HALF, LANES),
            vmem(ROWS, HALF, LANES), half(HALF, 2048), half(HALF, 2048),
            vmem(ROWS, LANES, LANES), vmem(S, S),
            vmem(2, CHIPS, 10, LANES), vmem(2, CHIPS, 10, LANES), vmem(2, CHIPS, 10, LANES),
            vmem(2, ROWS, 2, HALF, LANES),
            half(S, 2048), half(S, 2048),
            half(S, S), half(S, S), vmem(S, LANES),
            vmem(S, S), vmem(S, LANES),
            vmem(HALF, LANES), vmem(2, HALF, LANES),
            vmem(2, S, S), vmem(S, S),
            vmem(ROWS, 20, S), vmem(ROWS, 20, S), vmem(ROWS, 20, S), vmem(S, S),
            vmem(HALF, 2 * LANES),
            vmem(2, ROWS, 3, 8, LANES), vmem(2, ROWS, 3, 8, LANES), vmem(2, 2, ROWS, 3, 8, LANES),
            vmem(ROWS, 20, S),
            dma((3,)), dma((2, 3)),
            dma((2, 2, 5, 3)), dma((2,)),
            dma(()), dma(()),
            dma((2, 2)), dma((2, 2)),
            dma(()), dma(()),
            dma((2,)), dma((2,)),
            dma((2, 2)), dma((2, 3)), dma((2, 3)),
        ],
        compiler_params=pltpu.CompilerParams(
            collective_id=0, has_side_effects=True, vmem_limit_bytes=48 * 2**20
        ),
        cost_estimate=pl.CostEstimate(flops=2 * 10**9, bytes_accessed=4 * 10**6, transcendentals=0),
    )(deltas, row_sketch.T, slab_sketch, core_sketch, slab_sketch_two, ranks)
    return jnp.transpose(core_t, (1, 2, 0))


def solution(mesh):
    in_specs = (
        P("fiber", "row", None),
        P("row", None),
        P("fiber", None),
        P(),
        P("fiber", None),
        P(),
    )
    out_specs = P("fiber", None, "row")
    return jax.shard_map(local, mesh=mesh, in_specs=in_specs, out_specs=out_specs, check_vma=False)
```

time: 1090 us -> 127 us (0.12)
  waiting for transfers between devices: 865 us -> 0 us
  other arithmetic: 166 us -> 0 us
  Pallas kernels: 0 us -> 121 us
  matrix products: 20 us -> 0 us
  between operations: 18.6 us -> 0.02 us
  local copies, waits for them, and re-layouts: 17.4 us -> 5.8 us
    psum x4 -> x0, waiting for transfers between devices: 620 us -> none  [the longest x2 226 us: orthonormal(): return cholesky_pass(block, lax.psum(gram_of(block), 'row'))]
    another operation x32 -> x0, other arithmetic: 161 us -> none  [the longest x21 102 us: cholesky_pass(): lower = jnp.linalg.cholesky(gram)]
    pallas_call x0 -> x1, Pallas kernels: none -> 121 us  [local(): pl.pallas_call(kernel, out_shape=jax.ShapeDtypeStruct((S // ROWS, 1, S),...]
    all_gather x2 -> x0, waiting for transfers between devices: 116 us -> none  [the longest x1 72.2 us: local(): lax.all_gather(row_sketch, 'row', axis=0, tiled=True)]
    unnamed x8 -> x0, waiting for transfers between devices: 114 us -> none
    dot_general x6 -> x0, matrix products: 15.8 us -> none  [the longest x1 4.86 us: local(): jnp.einsum('mpq,qs->mps', deltas, lax.all_gather(row_sketch, 'row', axis=...]
    all_to_all x1 -> x0, waiting for transfers between devices: 14.6 us -> none  [local(): lax.all_to_all(deltas, 'row', split_axis=2, concat_axis=1, tiled=True)]
  transfers between devices with their start and end apart: 8 -> 0, of which waited for: 8 -> 0; matrix products, arithmetic and copies ran while one was open for 1% -> 0% of each run, Pallas kernels for 0% -> 0%
where the time goes in v2:
time: 127 us; the launch traced here: 126 us
  Pallas kernels  121 us (95%)
  local copies, waits for them, and re-layouts  5.8 us (5%)
    pallas_call x1, Pallas kernels, local(): pl.pallas_call(kernel, out_shape=jax.ShapeDtypeStruct((S // ROWS, 1, S),...  121 us
    unnamed x13, local copies, waits for them, and re-layouts  5.8 us

profile of v2, /device:TPU:1, one launch (start us, length us, event | category | flops | bytes accessed | tf_op | source)
XLA Modules:
  0.0 126.5 jit_solution(272151096803554487)
XLA Ops:
  0.0 0.0 copy-start.3
  0.0 0.7 copy-done.3
  0.7 0.0 copy-start
  0.7 1.2 copy-done
  1.9 0.0 copy-start.1
  1.9 1.0 copy-done.1
  2.9 0.0 copy-start.2
  2.9 0.9 copy-done.2
  3.9 0.0 copy-start.4
  3.9 0.7 copy-done.4
  4.5 0.0 copy-start.5
  4.5 0.7 copy-done.5
  5.2 120.7 %shard_map.64 = f32[20,1,320]{2,1,0:T(1,128)S(1)} custom-call(f32[1,128,2048]{2,1,0:T(8,128)S(1)} %copy-done, f32[320,128]{1,0:T(8,128)S(1)} %bitcast.3, f32[1,320]{1,0:T(1,128)S(1)} %copy-done.3, f32[320,320]{1,0:T(8,128)S(1)} %copy-done.1, f32[1,320]{1,0:T(1,128)S(1)} %copy-done.4, s32[2]{0:T(128)S(1)} %copy-done.5), custom_call_target="tpu_custom_call" | custom-call | flops 2000000000 | bytes 4000000 | tf_op jit(solution)/shard_map/pallas_call | solution.py:429
  125.9 0.6 copy.8
Async XLA Ops:
  0.0 0.7 copy-start.3
  0.7 1.2 copy-start
  1.9 1.0 copy-start.1
  2.9 0.9 copy-start.2
  3.9 0.7 copy-start.4
  4.5 0.7 copy-start.5

commit v3 on v2

--- a/solution.py
+++ b/solution.py
@@ -86,12 +86,11 @@
     return outs
 
 
-def cholesky_inverse(g, x, done, beside):
+def cholesky_inverse(g, x, done, beside, before_last):
     lane = lax.broadcasted_iota(jnp.int32, (8, LANES), 1)
     sub = lax.broadcasted_iota(jnp.int32, (8, LANES), 0)
 
-    def step(index, carry):
-        beside(index)
+    def step(index, last=False):
         rows = [
             jnp.where(
                 lane < BLOCK,
@@ -102,22 +101,32 @@
         ]
         block = jnp.concatenate(factor_block(rows), axis=0)
         inverse = split(block[:, BLOCK:])
+        solved = stack3(inverse, split(x[:BLOCK, :]), (1, 0))
+        if last:
+            done[S - BLOCK :, :] = solved
+            return
+        done[pl.ds(pl.multiple_of(index * BLOCK, BLOCK), BLOCK), :] = solved
         upper = stack3(inverse, split(g[:BLOCK, :]), (1, 0))
-        solved = stack3(inverse, split(x[:BLOCK, :]), (1, 0))
-        done[pl.ds(pl.multiple_of(index * BLOCK, BLOCK), BLOCK), :] = solved
         rest = split(upper[:, BLOCK:])
         g[: S - BLOCK, : S - BLOCK] = g[BLOCK:, BLOCK:] - stack3(rest, rest, (0, 0))
         x[: S - BLOCK, :] = x[BLOCK:, :] - stack3(rest, split(solved), (0, 0))
+
+    def loop(index, carry):
+        beside(index)
+        step(index)
         return carry
 
-    lax.fori_loop(0, S // BLOCK, step, 0)
+    lax.fori_loop(0, S // BLOCK - 1, loop, 0)
+    before_last()
+    step(S // BLOCK - 1, last=True)
 
 
 def kernel(
-    d_hbm, rs_hbm, w_ref, cs_hbm, w2_ref, ranks_ref, out_ref,
+    d_hbm, rs_hbm, w_hbm, cs_hbm, w2_hbm, ranks_hbm, out_ref,
+    w_ref, w2_ref, ranks_ref,
     d_own, d_sib, d_high, d_low, w_own, w_sib, rst, rst_high, rst_low, regrouped, cs_ref,
     chunks, parts, sums, ys, y_high, y_low, cs_high, cs_low, w2_col,
-    g, pc, mixed_in, mixed_out, xi, winv, bt_out, bt_in, bt_all, bt, first_sum,
+    g, pc, projected, mixed_in, mixed_out, own_pair, xi, winv, bt_out, bt_in, bt_all, bt, first_sum,
     g_out, g_in, g_all, w_rows,
     in_sem, sib_sem, gather_recv, gather_send, pass_send, pass_recv,
     z_send, z_recv, re_send, re_recv, b_send, b_recv, own_sem, g_send, g_recv,
@@ -154,13 +163,15 @@
     fetch_rs = fetch(rs_hbm.at[half_of_core], rst.at[me], 0)
     fetch_d = fetch(d_hbm.at[0], d_own, 1)
     fetch_cs = fetch(cs_hbm, cs_ref, 2)
+    fetch_w = fetch(w_hbm, w_ref, 3)
+    fetch_later = [fetch(w2_hbm, w2_ref, 4), fetch(ranks_hbm, ranks_ref, 5)]
     peers = [(2 * z_peer(e) + core, me) for e in AWAY]
     peers += [(fiber, at(dx, dy)) for dx, dy in OTHERS]
-    peers += [(2 * z + other, at(dx, dy)) for dx, dy in OTHERS]
     peers += [sibling]
     barrier = pltpu.get_barrier_semaphore()
     for peer in peers:
         pl.semaphore_signal(barrier, inc=1, device_id=peer, device_id_type=MESH)
+    fetch_w.wait()
     w_t = jnp.broadcast_to(w_ref[...], (LANES, S)).T
     w_own[0], w_own[1] = w_t[:HALF], w_t[HALF:]
     fetch_rs.wait()
@@ -244,6 +255,8 @@
     def first_group(first, slots):
         if first == 0:
             fetch_cs.wait()
+            for copy in fetch_later:
+                copy.wait()
             cs_high[...], cs_low[...] = split(cs_ref[...].T)
             w2_col[...] = jnp.broadcast_to(w2_ref[...], (LANES, S)).T
             for copy in to_sibling:
@@ -281,12 +294,12 @@
     one = fiber_sum(first_sum[:, :LANES] * w_own[core] + first_sum[:, LANES:] * w_sib[...], 0)
 
     def to_pair(value, which):
-        ys[which, me, core] = value
-        ref = ys.at[which, me, core]
+        own_pair[which, core] = value
+        ref = own_pair.at[which, core]
         copy = remote(ref, ref, own_sem.at[0, which], own_sem.at[1, which], sibling)
         closing.append(copy.wait_send)
         copy.wait_recv()
-        return ys[which, me].reshape(S, LANES)
+        return own_pair[which].reshape(S, LANES)
 
     def gram_sum(block, which, beside):
         high, low = split(jnp.concatenate([block, jnp.zeros((LANES // 2, LANES), F32)], axis=0))
@@ -343,13 +356,14 @@
     )
     g[...] = identity
     xi[0], xi[1] = identity, identity
-    buf = ys.at[0]
+    buf = ys
     block_one = to_pair(one, 0)
+    ys[me] = own_pair[0]
     start, first, rest = gather(lambda slot, start, size: buf.at[slot, core, pl.ds(start, size)], 1)
     gram_sum(block_one, 0, (start, first))
 
     def pass_on(index):
-        @pl.when(index == 3)
+        @pl.when(index == 1)
         def _():
             for offsets in GROUPS:
                 rest(offsets)
@@ -357,17 +371,19 @@
                 ref = buf.at[at(dx, dy), core]
                 remote(ref, ref, pass_send, pass_recv, sibling)
 
-    cholesky_inverse(g, xi.at[0], winv, pass_on)
+    def project_one():
+        wait_bytes(buf.at[pl.ds(0, ROWS - 1), other], pass_recv)
+        wait_bytes(regrouped.at[pl.ds(0, ROWS - 1)], re_recv)
+        for j in range(ROWS):
+            here = slice(j * LANES, (j + 1) * LANES)
+            y_high[:, here], y_low[:, here] = split(buf[j].reshape(S, LANES))
+        slabs = split(regrouped[...].reshape(ROWS * LANES, LANES))
+        projected[...] = dot3((y_high[...], y_low[...]), slabs, (1, 0))
+
+    cholesky_inverse(g, xi.at[0], winv, pass_on, project_one)
     closing.append(lambda: wait_bytes(buf.at[pl.ds(0, ROWS - 1), core], pass_send))
-    wait_bytes(buf.at[pl.ds(0, ROWS - 1), other], pass_recv)
-    wait_bytes(regrouped.at[pl.ds(0, ROWS - 1)], re_recv)
-    for j in range(ROWS):
-        here = slice(j * LANES, (j + 1) * LANES)
-        y_high[:, here], y_low[:, here] = split(buf[j].reshape(S, LANES))
-    slabs = split(regrouped[...].reshape(ROWS * LANES, LANES))
-    projected = dot3((y_high[...], y_low[...]), slabs, (1, 0))
     index = lax.broadcasted_iota(jnp.int32, (S, LANES), 0)
-    pc[...] = jnp.where(index < ranks_ref[0], dot3(split(winv[...]), split(projected), (1, 0)), 0.0)
+    pc[...] = jnp.where(index < ranks_ref[0], dot3(split(winv[...]), split(projected[...]), (1, 0)), 0.0)
 
     pc_pair = split(pc[...])
     mixed = dot3((cs_high[...], cs_low[...]), pc_pair, (1, 0)) * w2_col[...]
@@ -405,7 +421,7 @@
             for close in closing:
                 close()
 
-    cholesky_inverse(g, xi.at[1], winv, add_up)
+    cholesky_inverse(g, xi.at[1], winv, add_up, nothing)
     wait_bytes(bt_all.at[pl.ds(0, ROWS - 1)], b_recv.at[1])
     for j in range(ROWS):
         bt[20 * j : 20 * j + 20, :] = bt_all[j]
@@ -424,31 +440,31 @@
     vmem = lambda *shape: pltpu.VMEM(shape, F32)
     half = lambda *shape: pltpu.VMEM(shape, BF16)
     dma = pltpu.SemaphoreType.DMA
-    in_vmem = pl.BlockSpec(memory_space=pltpu.VMEM)
     in_hbm = pl.BlockSpec(memory_space=pltpu.HBM)
     core_t = pl.pallas_call(
         kernel,
         out_shape=jax.ShapeDtypeStruct((S // ROWS, 1, S), F32),
-        in_specs=[in_hbm, in_hbm, in_vmem, in_hbm, in_vmem, pl.BlockSpec(memory_space=pltpu.SMEM)],
-        out_specs=in_vmem,
+        in_specs=[in_hbm] * 6,
+        out_specs=pl.BlockSpec(memory_space=pltpu.VMEM),
         scratch_shapes=[
+            vmem(1, S), vmem(1, S), pltpu.SMEM((2,), jnp.int32),
             vmem(LANES, 2048), vmem(LANES, 2048),
             half(2 * LANES, 2048), half(2 * LANES, 2048),
             vmem(2, HALF, LANES), vmem(HALF, LANES),
             vmem(ROWS, HALF, LANES), half(HALF, 2048), half(HALF, 2048),
             vmem(ROWS, LANES, LANES), vmem(S, S),
             vmem(2, CHIPS, 10, LANES), vmem(2, CHIPS, 10, LANES), vmem(2, CHIPS, 10, LANES),
-            vmem(2, ROWS, 2, HALF, LANES),
+            vmem(ROWS, 2, HALF, LANES),
             half(S, 2048), half(S, 2048),
             half(S, S), half(S, S), vmem(S, LANES),
-            vmem(S, S), vmem(S, LANES),
-            vmem(HALF, LANES), vmem(2, HALF, LANES),
+            vmem(S, S), vmem(S, LANES), vmem(S, LANES),
+            vmem(HALF, LANES), vmem(2, HALF, LANES), vmem(2, 2, HALF, LANES),
             vmem(2, S, S), vmem(S, S),
             vmem(ROWS, 20, S), vmem(ROWS, 20, S), vmem(ROWS, 20, S), vmem(S, S),
             vmem(HALF, 2 * LANES),
             vmem(2, ROWS, 3, 8, LANES), vmem(2, ROWS, 3, 8, LANES), vmem(2, 2, ROWS, 3, 8, LANES),
             vmem(ROWS, 20, S),
-            dma((3,)), dma((2, 3)),
+            dma((6,)), dma((2, 3)),
             dma((2, 2, 5, 3)), dma((2,)),
             dma(()), dma(()),
             dma((2, 2)), dma((2, 2)),
@@ -457,7 +473,7 @@
             dma((2, 2)), dma((2, 3)), dma((2, 3)),
         ],
         compiler_params=pltpu.CompilerParams(
-            collective_id=0, has_side_effects=True, vmem_limit_bytes=48 * 2**20
+            collective_id=0, has_side_effects=True, vmem_limit_bytes=62 * 2**20
         ),
         cost_estimate=pl.CostEstimate(flops=2 * 10**9, bytes_accessed=4 * 10**6, transcendentals=0),
     )(deltas, row_sketch.T, slab_sketch, core_sketch, slab_sketch_two, ranks)

time: 127 us -> 122 us (0.961)
  local copies, waits for them, and re-layouts: 5.8 us -> 1.38 us
    unnamed x13 -> x1, local copies, waits for them, and re-layouts: 5.8 us -> 1.38 us
where the time goes in v3:
time: 122 us
  Pallas kernels  121 us (99%)
  local copies, waits for them, and re-layouts  1.38 us (1%)
    pallas_call x1, Pallas kernels, local(): pl.pallas_call(kernel, out_shape=jax.ShapeDtypeStruct((S // ROWS, 1, S),...  121 us

profile of v3, /device:TPU:1, one launch (start us, length us, event | category | flops | bytes accessed | tf_op | source)
XLA Modules:
  0.0 122.1 jit_solution(1918746896281461833)
XLA Ops:
  0.0 120.7 %shard_map.64 = f32[20,1,320]{2,1,0:T(1,128)} custom-call(f32[1,128,2048]{2,1,0:T(8,128)} %d_hbm.1, f32[320,128]{1,0:T(8,128)} %bitcast.3, f32[1,320]{1,0:T(1,128)} %w_hbm.1, f32[320,320]{1,0:T(8,128)} %cs_hbm.1, f32[1,320]{1,0:T(1,128)} %w2_hbm.1, s32[2]{0:T(128)} %ranks_hbm.1), custom_call_target="tpu_custom_call" | custom-call | flops 2000000000 | bytes 4000000 | tf_op jit(solution)/shard_map/pallas_call | solution.py:444
  120.7 1.4 %copy.8 = f32[1,320,20]{1,0,2:T(1,128)} copy(f32[1,320,20]{1,0,2:T(1,128)} %bitcast.2) | data formatting | bytes 51200

commit v4 on v3

--- a/solution.py
+++ b/solution.py
@@ -125,11 +125,11 @@
     d_hbm, rs_hbm, w_hbm, cs_hbm, w2_hbm, ranks_hbm, out_ref,
     w_ref, w2_ref, ranks_ref,
     d_own, d_sib, d_high, d_low, w_own, w_sib, rst, rst_high, rst_low, regrouped, cs_ref,
-    chunks, parts, sums, ys, y_high, y_low, cs_high, cs_low, w2_col,
+    chunks, parts, sums, ys, ys_sib, y_high, y_low, cs_high, cs_low, w2_col,
     g, pc, projected, mixed_in, mixed_out, own_pair, xi, winv, bt_out, bt_in, bt_all, bt, first_sum,
-    g_out, g_in, g_all, w_rows,
+    g_out, g_in, g_all,
     in_sem, sib_sem, gather_recv, gather_send, pass_send, pass_recv,
-    z_send, z_recv, re_send, re_recv, b_send, b_recv, own_sem, g_send, g_recv,
+    z_send, z_recv, re_send, re_recv, b_send, b_recv, own_sem, g_send, g_recv, reach_sem,
 ):
     fiber, me = lax.axis_index("fiber"), lax.axis_index("row")
     z, core = lax.div(fiber, 2), lax.rem(fiber, 2)
@@ -160,13 +160,14 @@
         return copy
 
     half_of_core = pl.ds(pl.multiple_of(core * HALF, HALF), HALF)
+    half_of_sibling = pl.ds(pl.multiple_of(other * HALF, HALF), HALF)
     fetch_rs = fetch(rs_hbm.at[half_of_core], rst.at[me], 0)
     fetch_d = fetch(d_hbm.at[0], d_own, 1)
     fetch_cs = fetch(cs_hbm, cs_ref, 2)
     fetch_w = fetch(w_hbm, w_ref, 3)
     fetch_later = [fetch(w2_hbm, w2_ref, 4), fetch(ranks_hbm, ranks_ref, 5)]
-    peers = [(2 * z_peer(e) + core, me) for e in AWAY]
-    peers += [(fiber, at(dx, dy)) for dx, dy in OTHERS]
+    peers = [(fiber, at(dx, dy)) for dx, dy in OTHERS]
+    peers += [(2 * z_peer(e) + core, me) for e in (1, CHIPS - 1)]
     peers += [sibling]
     barrier = pltpu.get_barrier_semaphore()
     for peer in peers:
@@ -178,22 +179,41 @@
     fetch_d.wait()
     pl.semaphore_wait(barrier, len(peers))
 
+    def reach(step):
+        if step > 0:
+            pl.semaphore_wait(reach_sem.at[step - 1], 2)
+        if step < 3:
+            for e in (2**step, CHIPS - 2**step):
+                to = (2 * z_peer(e) + core, me)
+                pl.semaphore_signal(reach_sem.at[step], inc=1, device_id=to, device_id_type=MESH)
+
+    def drain():
+        while closing:
+            closing.pop(0)()
+
+    reach(0)
+
     def gather(buf, which):
         send = gather_send.at[which]
         closing.append(lambda: wait_bytes(rst.at[pl.ds(0, ROWS - 1)], send))
 
         def piece(s, slot):
             return buf(slot, s * SUB, SUB)
+
+        def receive(s, j, d):
+            if which == 1 and j > 0:
+                return gather_recv.at[1, 0, 1, 0]
+            return gather_recv.at[which, s, j, d - 1]
 
         def push(s, slot, axis, j):
             for d in (2, 1, 3):
                 ref = piece(s, slot)
                 to = at(d, 0) if axis == 0 else at(0, d)
-                remote(ref, ref, send, gather_recv.at[which, s, j, d - 1], (fiber, to))
+                remote(ref, ref, send, receive(s, j, d), (fiber, to))
 
         def arrived(s, ex, ey):
             near, last = (ex, ey) if s == 0 else (ey, ex)
-            sem = gather_recv.at[which, s, 1 + near, last - 1] if last else gather_recv.at[which, s, 0, near - 1]
+            sem = receive(s, 1 + near, last) if last else receive(s, 0, near)
             slot = at(-ex, -ey)
             wait_bytes(piece(s, slot), sem)
             if not last:
@@ -211,6 +231,9 @@
                     arrived(s, *((e, 0) if s == 0 else (0, e)))
 
         def rest(offsets):
+            if which == 1:
+                wait_bytes(rst.at[pl.ds(0, ROWS - SIDE)], receive(0, 1, 1))
+                return
             for ex, ey in offsets:
                 for s in range(2):
                     if (ex, ey)[1 - s]:
@@ -221,16 +244,15 @@
     def add_to(ref, first, value):
         ref[...] = value if first == 0 else ref[...] + value
 
-    def fiber_sum(value, which):
+    def fiber_sum(value, which, beside):
         for i in range(CHIPS):
             chunks[which, i] = value[10 * i : 10 * i + 10]
         sent, got = z_send.at[which], z_recv.at[which]
-        for i in range(2):
-            closing.append(lambda i=i: wait_bytes(parts.at[which, pl.ds(0, CHIPS - 1)], sent.at[i]))
         for e in AWAY:
             to = z_peer(e)
             remote(chunks.at[which, to], parts.at[which, z], sent.at[0], got.at[0], (2 * to + core, me))
         parts[which, z] = chunks[which, z]
+        beside()
         wait_bytes(parts.at[which, pl.ds(0, CHIPS - 1)], got.at[0])
         total = parts[which, 0]
         for i in range(1, CHIPS):
@@ -239,6 +261,8 @@
         for e in AWAY:
             to = z_peer(e)
             remote(sums.at[which, z], sums.at[which, z], sent.at[1], got.at[1], (2 * to + core, me))
+        for i in range(2):
+            closing.append(lambda i=i: wait_bytes(parts.at[which, pl.ds(0, CHIPS - 1)], sent.at[i]))
         wait_bytes(sums.at[which, pl.ds(0, CHIPS - 1)], got.at[1])
         return jnp.concatenate([sums[which, i] for i in range(CHIPS)], axis=0)
 
@@ -269,11 +293,6 @@
                     d_high[:LANES, here], d_low[:LANES, here] = split(d_own[:, cols])
                     d_high[LANES:, here], d_low[LANES:, here] = split(d_sib[:, cols])
                     i += 1
-        if first + len(slots) == ROWS:
-            for dx, dy in OTHERS:
-                to = at(dx, dy)
-                remote(d_own.at[:, columns(to)], regrouped.at[me], re_send, re_recv, (fiber, to))
-            closing.append(lambda: wait_bytes(regrouped.at[pl.ds(0, ROWS - 1)], re_send))
         for i, slot in enumerate(slots):
             here = slice((first + i) * LANES, (first + i + 1) * LANES)
             rst_high[:, here], rst_low[:, here] = split(rst[slot])
@@ -284,14 +303,23 @@
 
     start, first, rest = gather(lambda slot, start, size: rst.at[slot, pl.ds(start, size)], 0)
     start()
+    reach(1)
     first()
+    reach(2)
     count = 0
     for offsets in GROUPS:
         rest(offsets)
         first_group(count, [at(-ex, -ey) for ex, ey in offsets])
         count += len(offsets)
-    regrouped[me] = d_own[:, columns(me)]
-    one = fiber_sum(first_sum[:, :LANES] * w_own[core] + first_sum[:, LANES:] * w_sib[...], 0)
+    def regroup():
+        for dx, dy in OTHERS:
+            to = at(dx, dy)
+            remote(d_own.at[:, columns(to)], regrouped.at[me], re_send, re_recv, (fiber, to))
+        regrouped[me] = d_own[:, columns(me)]
+
+    reach(3)
+    one = fiber_sum(first_sum[:, :LANES] * w_own[core] + first_sum[:, LANES:] * w_sib[...], 0, regroup)
+    closing.append(lambda: wait_bytes(regrouped.at[pl.ds(0, ROWS - 1)], re_send))
 
     def to_pair(value, which):
         own_pair[which, core] = value
@@ -356,32 +384,29 @@
     )
     g[...] = identity
     xi[0], xi[1] = identity, identity
-    buf = ys
     block_one = to_pair(one, 0)
-    ys[me] = own_pair[0]
-    start, first, rest = gather(lambda slot, start, size: buf.at[slot, core, pl.ds(start, size)], 1)
+    ys[me] = one
+    start, first, rest = gather(lambda slot, start, size: ys.at[slot, pl.ds(start, size)], 1)
     gram_sum(block_one, 0, (start, first))
 
     def pass_on(index):
         @pl.when(index == 1)
         def _():
-            for offsets in GROUPS:
-                rest(offsets)
-            for dx, dy in OTHERS:
-                ref = buf.at[at(dx, dy), core]
-                remote(ref, ref, pass_send, pass_recv, sibling)
+            rest(None)
+            remote(ys, ys_sib, pass_send, pass_recv, sibling)
 
     def project_one():
-        wait_bytes(buf.at[pl.ds(0, ROWS - 1), other], pass_recv)
+        wait_bytes(ys_sib, pass_recv)
         wait_bytes(regrouped.at[pl.ds(0, ROWS - 1)], re_recv)
         for j in range(ROWS):
             here = slice(j * LANES, (j + 1) * LANES)
-            y_high[:, here], y_low[:, here] = split(buf[j].reshape(S, LANES))
+            y_high[half_of_core, here], y_low[half_of_core, here] = split(ys[j])
+            y_high[half_of_sibling, here], y_low[half_of_sibling, here] = split(ys_sib[j])
         slabs = split(regrouped[...].reshape(ROWS * LANES, LANES))
         projected[...] = dot3((y_high[...], y_low[...]), slabs, (1, 0))
 
     cholesky_inverse(g, xi.at[0], winv, pass_on, project_one)
-    closing.append(lambda: wait_bytes(buf.at[pl.ds(0, ROWS - 1), core], pass_send))
+    closing.append(lambda: wait_bytes(ys, pass_send))
     index = lax.broadcasted_iota(jnp.int32, (S, LANES), 0)
     pc[...] = jnp.where(index < ranks_ref[0], dot3(split(winv[...]), split(projected[...]), (1, 0)), 0.0)
 
@@ -391,12 +416,13 @@
     exchange = remote(mixed_out.at[other], mixed_in, sib_sem.at[0, 2], sib_sem.at[1, 2], sibling)
     closing.append(exchange.wait_send)
     exchange.wait_recv()
-    block_two = to_pair(fiber_sum(mixed_out[core] + mixed_in[...], 1), 1)
+    block_two = to_pair(fiber_sum(mixed_out[core] + mixed_in[...], 1, drain), 1)
 
     def nothing():
         pass
 
     def project_two():
+        drain()
         bt_part = dot3(split(block_two), pc_pair, (1, 1))
         for j in range(ROWS):
             bt_out[j] = bt_part[20 * j : 20 * j + 20]
@@ -418,20 +444,22 @@
             for dx, dy in OTHERS:
                 to = at(dx, dy)
                 remote(bt_all.at[me], bt_all.at[me], b_send.at[1], b_recv.at[1], (fiber, to))
-            for close in closing:
-                close()
-
-    cholesky_inverse(g, xi.at[1], winv, add_up, nothing)
-    wait_bytes(bt_all.at[pl.ds(0, ROWS - 1)], b_recv.at[1])
-    for j in range(ROWS):
-        bt[20 * j : 20 * j + 20, :] = bt_all[j]
-        w_rows[j] = winv[20 * j : 20 * j + 20, :]
-    mine = w_rows[me]
+
+    def assemble():
+        wait_bytes(bt_all.at[pl.ds(0, ROWS - 1)], b_recv.at[1])
+        for j in range(ROWS):
+            bt[20 * j : 20 * j + 20, :] = bt_all[j]
+
+    cholesky_inverse(g, xi.at[1], winv, add_up, assemble)
+    odd = lax.rem(me, 2)
+    window = winv[pl.ds(pl.multiple_of(20 * me - 4 * odd, 8), 24), :]
+    mine = jnp.where(odd == 0, window[:20], window[4:])
     keep = lax.broadcasted_iota(jnp.int32, mine.shape, 0) + 20 * me < ranks_ref[1]
     mine = jnp.where(keep, mine, 0.0)
     core_t = dot3(split(mine), split(bt[...]), (1, 0))
     for i in range(S // ROWS):
         out_ref[i] = core_t[i : i + 1]
+    drain()
     for i in range(2):
         wait_bytes(bt_all.at[pl.ds(0, ROWS - 1)], b_send.at[i])
 
@@ -454,7 +482,7 @@
             vmem(ROWS, HALF, LANES), half(HALF, 2048), half(HALF, 2048),
             vmem(ROWS, LANES, LANES), vmem(S, S),
             vmem(2, CHIPS, 10, LANES), vmem(2, CHIPS, 10, LANES), vmem(2, CHIPS, 10, LANES),
-            vmem(ROWS, 2, HALF, LANES),
+            vmem(ROWS, HALF, LANES), vmem(ROWS, HALF, LANES),
             half(S, 2048), half(S, 2048),
             half(S, S), half(S, S), vmem(S, LANES),
             vmem(S, S), vmem(S, LANES), vmem(S, LANES),
@@ -463,7 +491,6 @@
             vmem(ROWS, 20, S), vmem(ROWS, 20, S), vmem(ROWS, 20, S), vmem(S, S),
             vmem(HALF, 2 * LANES),
             vmem(2, ROWS, 3, 8, LANES), vmem(2, ROWS, 3, 8, LANES), vmem(2, 2, ROWS, 3, 8, LANES),
-            vmem(ROWS, 20, S),
             dma((6,)), dma((2, 3)),
             dma((2, 2, 5, 3)), dma((2,)),
             dma(()), dma(()),
@@ -471,6 +498,7 @@
             dma(()), dma(()),
             dma((2,)), dma((2,)),
             dma((2, 2)), dma((2, 3)), dma((2, 3)),
+            pltpu.SemaphoreType.REGULAR((3,)),
         ],
         compiler_params=pltpu.CompilerParams(
             collective_id=0, has_side_effects=True, vmem_limit_bytes=62 * 2**20

time: 122 us -> 120 us (0.984)
  Pallas kernels: 121 us -> 119 us
    pallas_call x1, Pallas kernels: 121 us -> 119 us  [local(): pl.pallas_call(kernel, out_shape=jax.ShapeDtypeStruct((S // ROWS, 1, S),...]
where the time goes in v4:
time: 120 us
  Pallas kernels  119 us (99%)
  local copies, waits for them, and re-layouts  1.38 us (1%)
    pallas_call x1, Pallas kernels, local(): pl.pallas_call(kernel, out_shape=jax.ShapeDtypeStruct((S // ROWS, 1, S),...  119 us

profile of v4, /device:TPU:1, one launch (start us, length us, event | category | flops | bytes accessed | tf_op | source)
XLA Modules:
  0.0 119.9 jit_solution(4667913638894519904)
XLA Ops:
  0.0 118.5 %shard_map.64 = f32[20,1,320]{2,1,0:T(1,128)} custom-call(f32[1,128,2048]{2,1,0:T(8,128)} %d_hbm.1, f32[320,128]{1,0:T(8,128)} %bitcast.3, f32[1,320]{1,0:T(1,128)} %w_hbm.1, f32[320,320]{1,0:T(8,128)} %cs_hbm.1, f32[1,320]{1,0:T(1,128)} %w2_hbm.1, s32[2]{0:T(128)} %ranks_hbm.1), custom_call_target="tpu_custom_call" | custom-call | flops 2000000000 | bytes 4000000 | tf_op jit(solution)/shard_map/pallas_call | solution.py:472
  118.6 1.4 %copy.8 = f32[1,320,20]{1,0,2:T(1,128)} copy(f32[1,320,20]{1,0,2:T(1,128)} %bitcast.2) | data formatting | bytes 51200

commit v5 on v4

--- a/solution.py
+++ b/solution.py
@@ -316,6 +316,12 @@
             to = at(dx, dy)
             remote(d_own.at[:, columns(to)], regrouped.at[me], re_send, re_recv, (fiber, to))
         regrouped[me] = d_own[:, columns(me)]
+        square = (S, S)
+        identity = jnp.where(
+            lax.broadcasted_iota(jnp.int32, square, 0) == lax.broadcasted_iota(jnp.int32, square, 1), 1.0, 0.0
+        )
+        g[...] = identity
+        xi[0], xi[1] = identity, identity
 
     reach(3)
     one = fiber_sum(first_sum[:, :LANES] * w_own[core] + first_sum[:, LANES:] * w_sib[...], 0, regroup)
@@ -378,12 +384,6 @@
             if i < ROWS // 2:
                 g[2 * LANES + 8 * i : 2 * LANES + 8 * i + 8, 2 * LANES :] = g_all[which, 1, i, 2][:, : LANES // 2]
 
-    square = (S, S)
-    identity = jnp.where(
-        lax.broadcasted_iota(jnp.int32, square, 0) == lax.broadcasted_iota(jnp.int32, square, 1), 1.0, 0.0
-    )
-    g[...] = identity
-    xi[0], xi[1] = identity, identity
     block_one = to_pair(one, 0)
     ys[me] = one
     start, first, rest = gather(lambda slot, start, size: ys.at[slot, pl.ds(start, size)], 1)
@@ -426,13 +426,13 @@
         bt_part = dot3(split(block_two), pc_pair, (1, 1))
         for j in range(ROWS):
             bt_out[j] = bt_part[20 * j : 20 * j + 20]
+        for dx, dy in OTHERS:
+            to = at(dx, dy)
+            remote(bt_out.at[to], bt_in.at[me], b_send.at[0], b_recv.at[0], (fiber, to))
+        bt_in[me] = bt_out[me]
+
 
     gram_sum(block_two, 1, (nothing, project_two))
-    for dx, dy in OTHERS:
-        to = at(dx, dy)
-        remote(bt_out.at[to], bt_in.at[me], b_send.at[0], b_recv.at[0], (fiber, to))
-    bt_in[me] = bt_out[me]
-
     def add_up(index):
         @pl.when(index == 2)
         def _():

time: 120 us -> 119 us (level)
  Pallas kernels: 119 us -> 117 us
    pallas_call x1, Pallas kernels: 119 us -> 117 us  [local(): pl.pallas_call(kernel, out_shape=jax.ShapeDtypeStruct((S // ROWS, 1, S),...]
where the time goes in v5:
time: 119 us; the launch traced here: 118 us
  Pallas kernels  117 us (98%)
  local copies, waits for them, and re-layouts  1.38 us (1%)
    pallas_call x1, Pallas kernels, local(): pl.pallas_call(kernel, out_shape=jax.ShapeDtypeStruct((S // ROWS, 1, S),...  117 us

profile of v5, /device:TPU:1, one launch (start us, length us, event | category | flops | bytes accessed | tf_op | source)
XLA Modules:
  0.0 118.5 jit_solution(2848338781194650920)
XLA Ops:
  0.0 117.1 %shard_map.64 = f32[20,1,320]{2,1,0:T(1,128)} custom-call(f32[1,128,2048]{2,1,0:T(8,128)} %d_hbm.1, f32[320,128]{1,0:T(8,128)} %bitcast.3, f32[1,320]{1,0:T(1,128)} %w_hbm.1, f32[320,320]{1,0:T(8,128)} %cs_hbm.1, f32[1,320]{1,0:T(1,128)} %w2_hbm.1, s32[2]{0:T(128)} %ranks_hbm.1), custom_call_target="tpu_custom_call" | custom-call | flops 2000000000 | bytes 4000000 | tf_op jit(solution)/shard_map/pallas_call | solution.py:472
  117.1 1.4 %copy.8 = f32[1,320,20]{1,0,2:T(1,128)} copy(f32[1,320,20]{1,0,2:T(1,128)} %bitcast.2) | data formatting | bytes 51200

commit v6 on v5

--- a/solution.py
+++ b/solution.py
@@ -450,7 +450,8 @@
         for j in range(ROWS):
             bt[20 * j : 20 * j + 20, :] = bt_all[j]
 
-    cholesky_inverse(g, xi.at[1], winv, add_up, assemble)
+    cholesky_inverse(g, xi.at[1], winv, add_up, nothing)
+    assemble()
     odd = lax.rem(me, 2)
     window = winv[pl.ds(pl.multiple_of(20 * me - 4 * odd, 8), 24), :]
     mine = jnp.where(odd == 0, window[:20], window[4:])

time: 119 us -> 117 us (0.983)
  Pallas kernels: 117 us -> 115 us
    pallas_call x1, Pallas kernels: 117 us -> 115 us  [local(): pl.pallas_call(kernel, out_shape=jax.ShapeDtypeStruct((S // ROWS, 1, S),...]
where the time goes in v6:
time: 117 us
  Pallas kernels  115 us (98%)
  local copies, waits for them, and re-layouts  1.38 us (1%)
    pallas_call x1, Pallas kernels, local(): pl.pallas_call(kernel, out_shape=jax.ShapeDtypeStruct((S // ROWS, 1, S),...  115 us

profile of v6, /device:TPU:1, one launch (start us, length us, event | category | flops | bytes accessed | tf_op | source)
XLA Modules:
  0.0 116.9 jit_solution(10743863836120699532)
XLA Ops:
  0.0 115.5 %shard_map.64 = f32[20,1,320]{2,1,0:T(1,128)} custom-call(f32[1,128,2048]{2,1,0:T(8,128)} %d_hbm.1, f32[320,128]{1,0:T(8,128)} %bitcast.3, f32[1,320]{1,0:T(1,128)} %w_hbm.1, f32[320,320]{1,0:T(8,128)} %cs_hbm.1, f32[1,320]{1,0:T(1,128)} %w2_hbm.1, s32[2]{0:T(128)} %ranks_hbm.1), custom_call_target="tpu_custom_call" | custom-call | flops 2000000000 | bytes 4000000 | tf_op jit(solution)/shard_map/pallas_call | solution.py:473
  115.5 1.4 %copy.8 = f32[1,320,20]{1,0,2:T(1,128)} copy(f32[1,320,20]{1,0,2:T(1,128)} %bitcast.2) | data formatting | bytes 51200
